TPU v7x, 32 devices: a whole 2x2x4 slice. The times are simulated.
32 devices in a mesh: dp: 4 (over z), ctx: 4 (over y, core), tp: 2 (over x).
Axes of the slice: x: 2, y: 2, z: 4, core: 2. Of those that a mesh axis runs over, the one named last changes fastest.
Arguments:
- hidden_in: bfloat16 [12, 1024, 768], P('dp', 'ctx'), may hold values from -6 to 6
- doc_lengths: int32 [12, 18], P('dp'), may hold values from 0 to 800, as said below
- sticky_places: int32 [12, 256], P('dp'), may hold values from 0 to 1023
- attn_gain: float32 [768], replicated, may hold values from 0.5 to 1.5
- attn_shift: float32 [768], replicated, may hold values from -1.25 to 1.25
- qkv_weight: bfloat16 [768, 3, 768], P('dp', None, 'tp'), may hold values from -0.21875 to 0.21875
- qkv_bias: float32 [3, 768], P(None, 'tp'), may hold values from -1.25 to 1.25
- center_weight: float32 [12, 256], P('tp'), may hold values from -0.375 to 0.375
- spread_weight: float32 [12, 256], P('tp'), may hold values from -0.375 to 0.375
- out_weight: bfloat16 [768, 768], P('tp', 'dp'), may hold values from -0.625 to 0.625
- out_bias: float32 [768], replicated, may hold values from -1.25 to 1.25
- mlp_gain: float32 [768], replicated, may hold values from 0.5 to 1.5
- mlp_shift: float32 [768], replicated, may hold values from -1.25 to 1.25
- fc_weight: bfloat16 [768, 3072], P('dp', 'tp'), may hold values from -0.21875 to 0.21875
- fc_bias: float32 [3072], P('tp'), may hold values from -1.25 to 1.25
- proj_weight: bfloat16 [3072, 768], P('tp', 'dp'), may hold values from -0.109375 to 0.109375
- proj_bias: float32 [768], replicated, may hold values from -1.25 to 1.25
- cotangent: bfloat16 [12, 1024, 768], P('dp', 'ctx'), may hold values from -6 to 6
Outputs:
- block_out: bfloat16 [12, 1024, 768], P('dp', 'ctx')
- input_grad: bfloat16 [12, 1024, 768], P('dp', 'ctx')
- attn_gain_grad: float32 [768], replicated
- attn_shift_grad: float32 [768], replicated
- qkv_weight_grad: float32 [768, 3, 768], P('dp', None, 'tp')
- qkv_bias_grad: float32 [3, 768], P(None, 'tp')
- center_weight_grad: float32 [12, 256], P('tp')
- spread_weight_grad: float32 [12, 256], P('tp')
- out_weight_grad: float32 [768, 768], P('tp', 'dp')
- out_bias_grad: float32 [768], replicated
- mlp_gain_grad: float32 [768], replicated
- mlp_shift_grad: float32 [768], replicated
- fc_weight_grad: float32 [768, 3072], P('dp', 'tp')
- fc_bias_grad: float32 [3072], P('tp')
- proj_weight_grad: float32 [3072, 768], P('tp', 'dp')
- proj_bias_grad: float32 [768], replicated
Inputs may be any that keep to these rules, and one draw needn't show every extreme that they name: `doc_lengths`: the entries of one sequence sum to 1024; zero entries are empty documents.
All inputs are finite; a program needn't handle non-finite values.
Results may differ from a plain program's by a relative error of at most 0.015.
The roundings to bfloat16 on the way count: a program that leaves them out, or rounds other values in their place, can miss the bound.
Values may be sent and summed in bfloat16 or wider, within the bound.
A program may use at most 128 MiB of HBM per device.

v0:
```python
import jax
import jax.numpy as jnp
from jax import lax
from jax.sharding import PartitionSpec as P

DH = 64
WINDOW = 512


highest = lax.Precision.HIGHEST
eps_norm = 1e-05
ridge_term = 0.5
spread_scale = 0.02


def passed_along(block, axis, distance):
    devices = range(lax.axis_size(axis))
    route = [(i - distance, i) for i in devices if i - distance in devices]
    return lax.ppermute(block, axis, route)


def layer_norm(values, gain_vec, shift_vec):
    mean_value = jnp.mean(values, axis=-1, keepdims=True)
    centred = values - mean_value
    variance = jnp.mean(centred * centred, axis=-1, keepdims=True)
    return centred * lax.rsqrt(variance + eps_norm) * gain_vec + shift_vec


def gelu_tanh(values):
    return (
        0.5
        * values
        * (1.0 + jnp.tanh(0.7978845608028654 * (values + 0.044715 * values * values * values)))
    )


def softplus_smooth(values):
    return jnp.log1p(jnp.exp(values))


def ridge_fit(basis_count, sample_count):
    centers = (jnp.arange(basis_count, dtype=jnp.float32) + 0.5) / basis_count
    sample_times = (jnp.arange(sample_count, dtype=jnp.float32) + 0.5) / sample_count
    basis_width = 1.0 / basis_count
    design = jnp.exp(
        -jnp.square(sample_times[None, :] - centers[:, None]) / (2.0 * basis_width * basis_width)
    )
    gram_matrix = jnp.dot(design, design.T, precision=highest) + ridge_term * jnp.eye(
        basis_count, dtype=jnp.float32
    )
    factor = jnp.linalg.cholesky(gram_matrix)
    return jax.scipy.linalg.cho_solve((factor, True), design)


def memory_reach(mem_scores, center_weight, spread_weight):
    basis_count = mem_scores.shape[-1]
    centers = (jnp.arange(basis_count, dtype=jnp.float32) + 0.5) / basis_count
    basis_width = 1.0 / basis_count
    center_logit = jnp.einsum("...hqj,hj->...hq", mem_scores, center_weight, precision=highest)
    spread_logit = jnp.einsum("...hqj,hj->...hq", mem_scores, spread_weight, precision=highest)
    middle = jax.nn.sigmoid(center_logit)[..., None]
    variance = (spread_scale * softplus_smooth(spread_logit) + basis_width * basis_width)[..., None]
    return (
        basis_width
        * lax.rsqrt(variance)
        * jnp.exp(-jnp.square(middle - centers) / (2.0 * variance))
    )


def segment_ids(doc_ends, positions):
    return jnp.sum(
        (doc_ends[:, None, :] <= positions[None, :, None]).astype(jnp.int32),
        axis=2,
        dtype=jnp.int32,
    )


def masked_scores(queries, key_rows, allowed):
    raw_scores = jnp.einsum(
        "qhd,khd->hqk", queries, key_rows, preferred_element_type=jnp.float32
    ) * DH ** (-0.5)
    return jnp.where(allowed[None], raw_scores, -1e30)


def attend(sequence_item):
    queries, key_rows, value_rows, allowed = sequence_item
    masked = masked_scores(queries, key_rows, allowed)
    row_max = jnp.max(masked, axis=-1, keepdims=True)
    exp_terms = jnp.exp(masked - row_max)
    row_total = jnp.sum(exp_terms, axis=-1, keepdims=True)
    shares = exp_terms / row_total
    local_out = jnp.einsum(
        "hqk,khd->qhd", shares.astype(jnp.bfloat16), value_rows, preferred_element_type=jnp.float32
    )
    return (local_out, row_max + jnp.log(row_total))


def attend_back(sequence_item):
    queries, key_rows, value_rows, allowed, log_total, grad_mixed = sequence_item
    masked = masked_scores(queries, key_rows, allowed)
    shares = jnp.exp(masked - log_total)
    grad_shares = jnp.einsum(
        "qhd,khd->hqk", grad_mixed, value_rows, preferred_element_type=jnp.float32
    )
    grad_scores = (
        shares * (grad_shares - jnp.sum(shares * grad_shares, axis=-1, keepdims=True))
    ).astype(jnp.bfloat16)
    grad_queries = jnp.einsum(
        "hqk,khd->qhd", grad_scores, key_rows, preferred_element_type=jnp.float32
    ) * DH ** (-0.5)
    grad_keys = jnp.einsum(
        "hqk,qhd->khd", grad_scores, queries, preferred_element_type=jnp.float32
    ) * DH ** (-0.5)
    grad_values = jnp.einsum(
        "hqk,qhd->khd", shares.astype(jnp.bfloat16), grad_mixed, preferred_element_type=jnp.float32
    )
    return (grad_queries, grad_keys, grad_values)


def per_device(
    hidden_in,
    doc_lengths,
    sticky_places,
    attn_gain,
    attn_shift,
    qkv_weight,
    qkv_bias,
    center_weight,
    spread_weight,
    out_weight,
    out_bias,
    mlp_gain,
    mlp_shift,
    fc_weight,
    fc_bias,
    proj_weight,
    proj_bias,
    cotangent,
):
    seq_count, block_rows, model_width = hidden_in.shape
    ctx_place = lax.axis_index("ctx")
    length = block_rows * lax.axis_size("ctx")
    head_count = center_weight.shape[0]
    basis_count = center_weight.shape[1]
    sticky_count = sticky_places.shape[1]
    head_width = qkv_bias.shape[1]
    score_scale = DH ** (-0.5)
    qkv_full, out_full, fc_full, proj_full = (
        lax.all_gather(qkv_weight, "dp", axis=0, tiled=True),
        lax.all_gather(out_weight, "dp", axis=1, tiled=True),
        lax.all_gather(fc_weight, "dp", axis=0, tiled=True),
        lax.all_gather(proj_weight, "dp", axis=1, tiled=True),
    )
    positions = ctx_place * block_rows + jnp.arange(block_rows, dtype=jnp.int32)
    key_positions = (ctx_place - 2) * block_rows + jnp.arange(3 * block_rows, dtype=jnp.int32)
    doc_ends = jnp.cumsum(doc_lengths, axis=1, dtype=jnp.int32)
    query_docs = segment_ids(doc_ends, positions)
    key_docs = segment_ids(doc_ends, key_positions)
    allowed = (
        (key_positions[None, None, :] <= positions[None, :, None])
        & (positions[None, :, None] - key_positions[None, None, :] < WINDOW)
        & (key_positions[None, None, :] >= 0)
        & (query_docs[:, :, None] == key_docs[:, None, :])
    )
    inputs_wide = hidden_in.astype(jnp.float32)
    normed, norm_pull = jax.vjp(layer_norm, inputs_wide, attn_gain, attn_shift)
    normed_low = normed.astype(jnp.bfloat16)
    qkv = (
        jnp.einsum("sbd,dke->sbke", normed_low, qkv_full, preferred_element_type=jnp.float32)
        + qkv_bias
    ).astype(jnp.bfloat16)
    queries = qkv[:, :, 0].reshape(seq_count, block_rows, head_count, DH)
    own_pair = qkv[:, :, 1:]
    pair_parts = []
    for offset in (2, 1):
        pair_parts.append(passed_along(own_pair, "ctx", offset))
    pair_rows = jnp.concatenate(pair_parts + [own_pair], axis=1)
    key_rows = pair_rows[:, :, 0].reshape(seq_count, 3 * block_rows, head_count, DH)
    value_rows = pair_rows[:, :, 1].reshape(seq_count, 3 * block_rows, head_count, DH)
    local_out, log_total = lax.map(attend, (queries, key_rows, value_rows, allowed))
    uniform = jnp.arange(sticky_count, dtype=jnp.int32) * length // sticky_count + length // (
        2 * sticky_count
    )
    all_places = jnp.concatenate(
        [sticky_places, jnp.broadcast_to(uniform, sticky_places.shape)], axis=1
    )
    local_index = all_places - ctx_place * block_rows
    inside = (local_index >= 0) & (local_index < block_rows)
    kv_flat = own_pair.reshape(seq_count, block_rows, 2 * head_width)
    sampled = jnp.take_along_axis(
        kv_flat, jnp.clip(local_index, 0, block_rows - 1)[:, :, None], axis=1
    )
    sampled = jnp.where(inside[:, :, None], sampled, jnp.zeros_like(sampled))
    fit_low = ridge_fit(basis_count, 2 * sticky_count).astype(jnp.bfloat16)
    partial_memory = jnp.einsum("bm,smc->sbc", fit_low, sampled, preferred_element_type=jnp.float32)
    memory = lax.psum(partial_memory, "ctx").astype(jnp.bfloat16)
    mem_keys = memory[:, :, :head_width].reshape(seq_count, basis_count, head_count, DH)
    mem_values = memory[:, :, head_width:].reshape(seq_count, basis_count, head_count, DH)
    mem_scores = (
        jnp.einsum("sqhd,sbhd->shqb", queries, mem_keys, preferred_element_type=jnp.float32)
        * score_scale
    )
    reach_weights, reach_pull = jax.vjp(memory_reach, mem_scores, center_weight, spread_weight)
    reach_low = reach_weights.astype(jnp.bfloat16)
    recalled = jnp.einsum(
        "shqb,sbhd->sqhd", reach_low, mem_values, preferred_element_type=jnp.float32
    )
    mixed_heads = (
        (local_out + recalled).astype(jnp.bfloat16).reshape(seq_count, block_rows, head_width)
    )
    attn_part = jnp.einsum("sbe,ed->sbd", mixed_heads, out_full, preferred_element_type=jnp.float32)
    attn_sum = lax.psum(attn_part, "tp")
    residual = inputs_wide + attn_sum + out_bias
    mlp_normed, mlp_pull = jax.vjp(layer_norm, residual, mlp_gain, mlp_shift)
    mlp_low = mlp_normed.astype(jnp.bfloat16)
    pre_act = (
        jnp.einsum("sbd,df->sbf", mlp_low, fc_full, preferred_element_type=jnp.float32) + fc_bias
    )
    activated, gelu_pull = jax.vjp(gelu_tanh, pre_act)
    activated_low = activated.astype(jnp.bfloat16)
    mlp_part = jnp.einsum(
        "sbf,fd->sbd", activated_low, proj_full, preferred_element_type=jnp.float32
    )
    mlp_sum = lax.psum(mlp_part.astype(jnp.bfloat16), "tp").astype(jnp.float32)
    block_out = (residual + mlp_sum + proj_bias).astype(jnp.bfloat16)
    grad_out = cotangent.astype(jnp.float32)
    proj_grad = jnp.einsum(
        "sbf,sbd->fd", activated_low, cotangent, preferred_element_type=jnp.float32
    )
    proj_bias_grad = jnp.sum(grad_out, axis=(0, 1))
    grad_activated = jnp.einsum(
        "sbd,fd->sbf", cotangent, proj_full, preferred_element_type=jnp.float32
    )
    grad_pre = gelu_pull(grad_activated)[0].astype(jnp.bfloat16)
    fc_grad = jnp.einsum("sbd,sbf->df", mlp_low, grad_pre, preferred_element_type=jnp.float32)
    fc_bias_grad = jnp.sum(grad_pre, axis=(0, 1), dtype=jnp.float32)
    mlp_back_part = jnp.einsum("sbf,df->sbd", grad_pre, fc_full, preferred_element_type=jnp.float32)
    grad_mlp_normed = lax.psum(mlp_back_part, "tp")
    grad_residual, mlp_gain_grad, mlp_shift_grad = mlp_pull(grad_mlp_normed)
    grad_residual = grad_residual + grad_out
    out_bias_grad = jnp.sum(grad_residual, axis=(0, 1))
    grad_residual_low = grad_residual.astype(jnp.bfloat16)
    out_grad = jnp.einsum(
        "sbe,sbd->ed", mixed_heads, grad_residual_low, preferred_element_type=jnp.float32
    )
    grad_mixed = jnp.einsum(
        "sbd,ed->sbe", grad_residual_low, out_full, preferred_element_type=jnp.float32
    )
    grad_mixed = grad_mixed.astype(jnp.bfloat16).reshape(seq_count, block_rows, head_count, DH)
    grad_queries, grad_keys, grad_values = lax.map(
        attend_back, (queries, key_rows, value_rows, allowed, log_total, grad_mixed)
    )
    grad_reach = jnp.einsum(
        "sqhd,sbhd->shqb", grad_mixed, mem_values, preferred_element_type=jnp.float32
    )
    grad_mem_values = jnp.einsum(
        "shqb,sqhd->sbhd", reach_low, grad_mixed, preferred_element_type=jnp.float32
    )
    grad_mem_scores, center_grad, spread_grad = reach_pull(grad_reach)
    grad_mem_scores = grad_mem_scores.astype(jnp.bfloat16)
    grad_queries = (
        grad_queries
        + jnp.einsum(
            "shqb,sbhd->sqhd", grad_mem_scores, mem_keys, preferred_element_type=jnp.float32
        )
        * score_scale
    )
    grad_mem_keys = (
        jnp.einsum("shqb,sqhd->sbhd", grad_mem_scores, queries, preferred_element_type=jnp.float32)
        * score_scale
    )
    grad_memory_part = jnp.concatenate(
        [
            grad_mem_keys.reshape(seq_count, basis_count, head_width),
            grad_mem_values.reshape(seq_count, basis_count, head_width),
        ],
        axis=2,
    )
    grad_memory = lax.psum(grad_memory_part.astype(jnp.bfloat16), "ctx")
    grad_sampled = jnp.einsum(
        "bm,sbc->smc", fit_low, grad_memory, preferred_element_type=jnp.float32
    )
    row_index = jnp.where(inside, local_index, block_rows)
    seq_index = jnp.arange(seq_count, dtype=jnp.int32)[:, None]
    grad_fit_rows = (
        jnp.zeros((seq_count, block_rows, 2 * head_width), jnp.float32)
        .at[seq_index, row_index]
        .add(grad_sampled, mode="drop")
    )
    grad_pair = jnp.stack(
        [
            grad_keys.reshape(seq_count, 3 * block_rows, head_width),
            grad_values.reshape(seq_count, 3 * block_rows, head_width),
        ],
        axis=2,
    )
    grad_own = grad_pair[:, 2 * block_rows :] + grad_fit_rows.reshape(
        seq_count, block_rows, 2, head_width
    )
    for offset in (2, 1):
        start_row = (2 - offset) * block_rows
        grad_own = grad_own + passed_along(
            grad_pair[:, start_row : start_row + block_rows].astype(jnp.bfloat16), "ctx", -offset
        ).astype(jnp.float32)
    grad_qkv = jnp.concatenate(
        [grad_queries.reshape(seq_count, block_rows, 1, head_width), grad_own], axis=2
    ).astype(jnp.bfloat16)
    qkv_grad = jnp.einsum("sbd,sbke->dke", normed_low, grad_qkv, preferred_element_type=jnp.float32)
    qkv_bias_grad = jnp.sum(grad_qkv, axis=(0, 1), dtype=jnp.float32)
    grad_normed = lax.psum(
        jnp.einsum("sbke,dke->sbd", grad_qkv, qkv_full, preferred_element_type=jnp.float32).astype(
            jnp.bfloat16
        ),
        "tp",
    ).astype(jnp.float32)
    grad_inputs, attn_gain_grad, attn_shift_grad = norm_pull(grad_normed)
    input_grad = (grad_inputs + grad_residual).astype(jnp.bfloat16)
    (
        attn_gain_grad,
        attn_shift_grad,
        qkv_bias_grad,
        center_grad,
        spread_grad,
        out_bias_grad,
        mlp_gain_grad,
        mlp_shift_grad,
        fc_bias_grad,
        proj_bias_grad,
    ) = lax.psum(
        (
            attn_gain_grad,
            attn_shift_grad,
            qkv_bias_grad,
            center_grad,
            spread_grad,
            out_bias_grad,
            mlp_gain_grad,
            mlp_shift_grad,
            fc_bias_grad,
            proj_bias_grad,
        ),
        ("dp", "ctx"),
    )
    shard_parts = (
        lax.psum_scatter(
            qkv_grad.astype(jnp.bfloat16), "dp", scatter_dimension=0, tiled=True
        ).astype(jnp.float32),
        lax.psum_scatter(
            out_grad.astype(jnp.bfloat16), "dp", scatter_dimension=1, tiled=True
        ).astype(jnp.float32),
        lax.psum_scatter(
            fc_grad.astype(jnp.bfloat16), "dp", scatter_dimension=0, tiled=True
        ).astype(jnp.float32),
        lax.psum_scatter(
            proj_grad.astype(jnp.bfloat16), "dp", scatter_dimension=1, tiled=True
        ).astype(jnp.float32),
    )
    qkv_grad, out_grad, fc_grad, proj_grad = (
        lax.psum(shard_parts[0].astype(jnp.bfloat16), "ctx").astype(jnp.float32),
        lax.psum(shard_parts[1].astype(jnp.bfloat16), "ctx").astype(jnp.float32),
        lax.psum(shard_parts[2].astype(jnp.bfloat16), "ctx").astype(jnp.float32),
        lax.psum(shard_parts[3].astype(jnp.bfloat16), "ctx").astype(jnp.float32),
    )
    return (
        block_out,
        input_grad,
        attn_gain_grad,
        attn_shift_grad,
        qkv_grad,
        qkv_bias_grad,
        center_grad,
        spread_grad,
        out_grad,
        out_bias_grad,
        mlp_gain_grad,
        mlp_shift_grad,
        fc_grad,
        fc_bias_grad,
        proj_grad,
        proj_bias_grad,
    )


def solution(mesh):
    in_specs = (
        P("dp", "ctx", None),
        P("dp", None),
        P("dp", None),
        P(),
        P(),
        P("dp", None, "tp"),
        P(None, "tp"),
        P("tp", None),
        P("tp", None),
        P("tp", "dp"),
        P(),
        P(),
        P(),
        P("dp", "tp"),
        P("tp"),
        P("tp", "dp"),
        P(),
        P("dp", "ctx", None),
    )
    out_specs = (
        P("dp", "ctx", None),
        P("dp", "ctx", None),
        P(),
        P(),
        P("dp", None, "tp"),
        P(None, "tp"),
        P("tp", None),
        P("tp", None),
        P("tp", "dp"),
        P(),
        P(),
        P(),
        P("dp", "tp"),
        P("tp"),
        P("tp", "dp"),
        P(),
    )
    return jax.shard_map(
        per_device, mesh=mesh, in_specs=in_specs, out_specs=out_specs, check_vma=False
    )
```

profile of v0, /device:TPU:0, one launch (start us, length us, event | category | flops | bytes accessed | tf_op | source)
XLA Modules:
  0.0 950.9 jit_solution(5538666288730868169)
XLA Ops:
  12.2 11.7 %cholesky.49 = f32[128,128]{1,0:T(8,128)S(1)} custom-call(f32[128,128]{1,0:T(8,128)S(1)} %cholesky.115), custom_call_target="Cholesky" | custom-call | tf_op jit(solution)/shard_map/jit(cholesky)/cholesky | solution.py:51
  24.0 9.8 %custom-call.18 = f32[1,128,128]{1,2,0:T(8,128)S(1)} custom-call(f32[1,128,128]{2,1,0:T(8,128)S(1)} %get-tuple-element.228), custom_call_target="InvertDiagBlocksLowerTriangular" | custom-call | tf_op jit(solution)/shard_map/jit(cholesky)/cholesky | solution.py:51
  34.3 11.7 %cholesky.103 = f32[128,128]{1,0:T(8,128)S(1)} custom-call(f32[128,128]{1,0:T(8,128)S(1)} %convolution_subtract_fusion.2), custom_call_target="Cholesky" | custom-call | tf_op jit(solution)/shard_map/jit(cholesky)/cholesky | solution.py:51
  52.1 18.9 %all_gather.13 = bf16[384,768]{0,1:T(8,128)(2,1)} all-gather(bf16[384,192]{0,1:T(8,128)(2,1)S(1)} %copy-done.33), channel_id=1, replica_groups=mesh['dp'=4,'ctx'=4,'tp'=2] {'dp'}, dimensions={1}, use_global_device_ids=true | all-gather | bytes 737280 | tf_op jit(solution)/shard_map/all_gather | solution.py:150
  71.0 19.7 %custom-call.19 = f32[2,128,128]{1,2,0:T(8,128)S(1)} custom-call(f32[2,128,128]{2,1,0:T(8,128)S(1)} %get-tuple-element.120), custom_call_target="InvertDiagBlocksLowerTriangular" | custom-call | tf_op jit(solution)/shard_map/jit(_cho_solve)/triangular_solve | solution.py:52
  110.3 20.7 %gather_fusion = bf16[1536,768]{1,0:T(8,128)(2,1)} fusion(bf16[3,256,768]{2,1,0:T(8,128)(2,1)S(1)} %copy.90, s32[1536]{0:T(1024)S(1)} %reshape.452), kind=kCustom, calls=%fused_computation | custom fusion | bytes 4730880 | tf_op jit(solution)/shard_map/jit(take_along_axis)/gather | solution.py:190
  139.2 45.0 %all-reduce.20 = bf16[3,256,768]{1,2,0:T(8,128)(2,1)S(1)} all-reduce(f32[3,256,768]{1,2,0:T(8,128)} %fusion.125), channel_id=1, replica_groups=mesh['dp'=4,'ctx'=4,'tp'=2] {'ctx'}, use_global_device_ids=true, to_apply=%region_13.14 | all-reduce | flops 589824 | bytes 3538944 | tf_op jit(solution)/shard_map/psum | solution.py:196
  207.4 22.1 %while.27 = (s32[]{:T(128)}, f32[3,256,6,64]{1,3,2,0:T(8,128)}, f32[3,6,256,1]{2,1,3,0:T(8,128)}, bf16[3,768,6,64]{1,3,2,0:T(8,128)(2,1)}, pred[3,256,768]{2,1,0...) while((s32[]{:T(128)}, f32[3,256,6,64]{1,3,2,0:T(8,128)}, ...), condition=%wide.region_8.9_spmd, body=%wide.region_5.8_spmd.sunk | while | flops 316144128 | bytes 16961636 | solution.py:180
  237.1 69.9 %all-reduce.11.cloned.1.call-done = f32[3,256,768]{2,1,0:T(8,128)} async-done(((f32[3,256,768]{2,1,0:T(8,128)}), f32[3,256,768]{2,1,0:T(8,128)}) %all-reduce.11.cloned.1.call-update) | async-done | bytes 2359312 | tf_op jit(solution)/shard_map/psum | solution.py:212
  311.5 47.6 %all-gather.6.cloned.1.call-done = bf16[768,1536]{1,0:T(8,128)(2,1)} async-done(((bf16[192,1536]{1,0:T(8,128)(2,1)}), bf16[768,1536]{1,0:T(8,128)(2,1)}) %all-gather.6.cloned.1.call-update) | async-done | bytes 2359312 | tf_op jit(solution)/shard_map/all_gather | solution.py:151
  359.1 6.7 fusion.105
  365.8 44.1 %all-gather.8.cloned.1.call-done = bf16[1536,768]{0,1:T(8,128)(2,1)} async-done(((bf16[1536,192]{0,1:T(8,128)(2,1)}), bf16[1536,768]{0,1:T(8,128)(2,1)}) %all-gather.8.cloned.1.call-update) | async-done | bytes 2359312 | tf_op jit(solution)/shard_map/all_gather | solution.py:152
  410.0 8.5 convert_reduce_fusion
  427.2 63.6 %all-reduce.13.cloned.1.call-done = f32[3,256,768]{2,1,0:T(8,128)} async-done(((f32[3,256,768]{2,1,0:T(8,128)}), f32[3,256,768]{2,1,0:T(8,128)}) %all-reduce.13.cloned.1.call-update) | async-done | bytes 2359312 | tf_op jit(solution)/shard_map/psum | solution.py:238
  505.5 4.4 fusion.61
  511.1 38.3 %while.28 = (s32[]{:T(128)}, f32[3,256,6,64]{1,3,2,0:T(8,128)}, f32[3,768,6,64]{1,3,2,0:T(8,128)}, f32[3,768,6,64]{1,3,2,0:T(8,128)}, bf16[3,768,6,64]{1,3,2,0:T...) while((s32[]{:T(128)}, f32[3,256,6,64]{1,3,2,0:T(8,128)}, ...), condition=%wide.region_23.24_spmd, body=%wide.region_21.23_spmd.sunk | while | flops 773061120 | bytes 44092568 | solution.py:250
  549.5 5.2 copy.97
  558.6 5.2 copy.96
  579.7 27.8 %all-reduce.15.cloned.1.call-done = bf16[3,256,768]{2,1,0:T(8,128)(2,1)} async-done(((bf16[3,256,768]{2,1,0:T(8,128)(2,1)}), bf16[3,256,768]{2,1,0:T(8,128)(2,1)}) %all-reduce.15.cloned.1.call-update) | async-done | bytes 1179664 | tf_op jit(solution)/shard_map/psum | solution.py:279
  611.9 12.8 %scatter_custom_fusion = f32[768,768]{1,0:T(8,128)} fusion(s32[1536]{0:T(1024)} %reshape.458, f32[1536,768]{1,0:T(8,128)} %bitcast.341, f32[]{:T(128)} %constant.214.clone.1), kind=kCustom, calls=%fused_computation.193 | custom fusion | flops 1179648 | bytes 2359808
  638.1 5.5 bitcast_convert_fusion.1
  644.3 6.5 bitcast_convert_fusion
  651.5 4.7 bitcast_convert_fusion.2
  656.5 4.7 fusion.70
  661.8 4.9 fusion.72
  668.2 35.3 %all-reduce.19.cloned.1.call-done = (bf16[3,256,768]{2,1,0:T(8,128)(2,1)}, bf16[3,256,768]{2,1,0:T(8,128)(2,1)}) async-done(((bf16[3,256,768]{2,1,0:T(8,128)(2,1)}, bf16[3,256,768]{2,1,0:T(8,128)(2,1)}), (bf16[3,256,768]{2,1,0:T(8,128)(2,1)}, bf16[3,256,768]{2,1,0:T(8,128)(2,1)})) %all-reduce.19.cloned.1.call-update) | async-done | bytes 2359312 | tf_op jit(solution)/shard_map/psum | solution.py:224
  709.0 19.4 %reduce-scatter.7.cloned.1.call-done = bf16[384,192]{0,1:T(8,128)(2,1)} async-done(((bf16[384,768]{0,1:T(8,128)(2,1)}), bf16[384,192]{0,1:T(8,128)(2,1)}) %reduce-scatter.7.cloned.1.call-update) | async-done | bytes 147472 | tf_op jit(solution)/shard_map/reduce_scatter | solution.py:348
  728.4 48.9 %reduce-scatter.9.cloned.1.call-done = bf16[192,1536]{1,0:T(8,128)(2,1)} async-done(((bf16[768,1536]{1,0:T(8,128)(2,1)}), bf16[192,1536]{1,0:T(8,128)(2,1)}) %reduce-scatter.9.cloned.1.call-update) | async-done | bytes 589840 | tf_op jit(solution)/shard_map/reduce_scatter | solution.py:351
  777.3 49.8 %reduce-scatter.11.cloned.1.call-done = bf16[1536,192]{0,1:T(8,128)(2,1)} async-done(((bf16[1536,768]{0,1:T(8,128)(2,1)}), bf16[1536,192]{0,1:T(8,128)(2,1)}) %reduce-scatter.11.cloned.1.call-update) | async-done | bytes 589840 | tf_op jit(solution)/shard_map/reduce_scatter | solution.py:354
  827.1 40.4 %reduce-scatter.5.cloned.1.call-done = bf16[192,3,384]{2,0,1:T(8,128)(2,1)} async-done(((bf16[768,3,384]{2,0,1:T(8,128)(2,1)}), bf16[192,3,384]{2,0,1:T(8,128)(2,1)}) %reduce-scatter.5.cloned.1.call-update) | async-done | bytes 442384 | tf_op jit(solution)/shard_map/reduce_scatter | solution.py:345
  868.2 4.4 convert_reduce_fusion.4
  872.6 61.4 %all-reduce.1 = (f32[768]{0:T(1024)}, f32[768]{0:T(1024)}, f32[3,384]{1,0:T(4,128)}, f32[6,256]{1,0:T(8,128)}, f32[6,256]{1,0:T(8,128)}, /*index=5*/f32[768]{0:T...) all-reduce(f32[768]{0:T(1024)} %get-tuple-element.143, ...), channel_id=1, replica_groups=mesh['dp'=4,'ctx'=4,'tp'=2] {'dp','ctx'}, use_global_device_ids=true, to_apply=%region_33.34 | all-reduce | flops 10368 | bytes 82944 | tf_op jit(solution)/shard_map/psum | solution.py:329
  (355 shorter events, 218.2 us)
Async XLA Ops:
  7.2 87.8 %all-gather.4.cloned.1.call-start = ((), (), s32[]{:S(2)}) async-start(), calls=%async_computation.4 | async-start | bytes 2211840 | tf_op jit(solution)/shard_map/all_gather | solution.py:149
  7.9 299.0 %all-reduce.11.cloned.1.call-start = ((), (), s32[]{:S(2)}) async-start(), calls=%async_computation.5 | async-start | bytes 4718592 | tf_op jit(solution)/shard_map/psum | solution.py:212
  8.0 221.6 %copy-start.65 = (f32[256]{0:T(256)}, f32[256]{0:T(256)S(1)}, u32[]{:S(2)}) copy-start(f32[256]{0:T(256)S(1)} %add_multiply_fusion.1) | copy-start | bytes 3076
  10.5 84.5 %copy-start.34 = (f32[3,256]{1,0:T(4,128)}, f32[3,256]{1,0:T(4,128)S(1)}, u32[]{:S(2)}) copy-start(f32[3,256]{1,0:T(4,128)S(1)} %broadcast_multiply_fusion.2) | copy-start | bytes 9220
  10.9 79.8 %copy-start.46 = (f32[3,256]{1,0:T(4,128)}, f32[3,256]{1,0:T(4,128)S(1)}, u32[]{:S(2)}) copy-start(f32[3,256]{1,0:T(4,128)S(1)} %fusion.86) | copy-start | bytes 9220
  11.2 40.9 %copy-start.33 = (bf16[384,192]{0,1:T(8,128)(2,1)S(1)}, bf16[384,192]{0,1:T(8,128)(2,1)}, u32[]{:S(2)}) copy-start(bf16[384,192]{0,1:T(8,128)(2,1)} %param.31) | copy-start | bytes 442372
  12.0 59.0 %copy-start.57 = (s32[3,256]{1,0:T(4,128)S(1)}, s32[3,256]{1,0:T(4,128)}, u32[]{:S(2)}) copy-start(s32[3,256]{1,0:T(4,128)} %param.24) | copy-start | bytes 9220
  92.9 42.4 %copy-start.27 = (bf16[128,512]{1,0:T(8,128)(2,1)}, bf16[128,512]{1,0:T(8,128)(2,1)S(1)}, u32[]{:S(2)}) copy-start(bf16[128,512]{1,0:T(8,128)(2,1)S(1)} %get-tuple-element.237) | copy-start | bytes 393220
  93.7 41.6 %copy-start.25 = (bf16[128,512]{1,0:T(8,128)(2,1)}, bf16[128,512]{1,0:T(8,128)(2,1)S(1)}, u32[]{:S(2)}) copy-start(bf16[128,512]{1,0:T(8,128)(2,1)S(1)} %convolution_convert_fusion.1) | copy-start | bytes 393220
  102.0 93.4 %collective-permute-start.1 = (bf16[3,256,2,384]{3,1,2,0:T(8,128)(2,1)}, bf16[3,256,2,384]{3,1,2,0:T(8,128)(2,1)}, u32[]{:S(2)}, u32[]{:S(2)}) collective-permute-start(bf16[3,256,2,384]{3,1,2,0:T(8,128)(2,1)} %slice.113), channel_id=1, source_target_pairs={{0,2},{2,4},{4,6},{1,3},{3,5},{5,7},{8,10},{10,12},{12,14},{9,11},... | collective-permute-start | bytes 3538952 | tf_op jit(solution)/shard_map/ppermute | solution.py:19
  104.4 91.0 %collective-permute-start = (bf16[3,256,2,384]{3,1,2,0:T(8,128)(2,1)}, bf16[3,256,2,384]{3,1,2,0:T(8,128)(2,1)}, u32[]{:S(2)}, u32[]{:S(2)}) collective-permute-start(bf16[3,256,2,384]{3,1,2,0:T(8,128)(2,1)} %slice.113), channel_id=1, source_target_pairs={{0,4},{2,6},{1,5},{3,7},{8,12},{10,14},{9,13},{11,15},{16,20},{18,... | collective-permute-start | bytes 3538952 | tf_op jit(solution)/shard_map/ppermute | solution.py:19
  235.7 71.3 %copy-start.64 = (f32[768]{0:T(1024)S(1)}, f32[768]{0:T(1024)}, u32[]{:S(2)}) copy-start(f32[768]{0:T(1024)} %param.32) | copy-start | bytes 9220
  235.7 123.4 %all-gather.6.cloned.1.call-start = ((), (), s32[]{:S(2)}) async-start(), calls=%async_computation.6 | async-start | bytes 2949120 | tf_op jit(solution)/shard_map/all_gather | solution.py:151
  236.5 173.5 %all-gather.8.cloned.1.call-start = ((), (), s32[]{:S(2)}) async-start(), calls=%async_computation.7 | async-start | bytes 2949120 | tf_op jit(solution)/shard_map/all_gather | solution.py:152
  237.0 253.8 %all-reduce.13.cloned.1.call-start = ((), (), s32[]{:S(2)}) async-start(), calls=%async_computation.8 | async-start | bytes 4718592 | tf_op jit(solution)/shard_map/psum | solution.py:238
  410.0 9.9 %copy-start.68 = (bf16[768,1536]{1,0:T(8,128)(2,1)S(1)}, bf16[768,1536]{1,0:T(8,128)(2,1)}, u32[]{:S(2)}) copy-start(bf16[768,1536]{1,0:T(8,128)(2,1)} %all-gather.6.cloned.1.call-done) | copy-start | bytes 7077892
  423.3 184.3 %all-reduce.15.cloned.1.call-start = ((), (), s32[]{:S(2)}) async-start(), calls=%async_computation.9 | async-start | bytes 2359296 | tf_op jit(solution)/shard_map/psum | solution.py:279
  427.2 67.6 %copy-start.48 = (f32[3,256]{1,0:T(4,128)S(1)}, f32[3,256]{1,0:T(4,128)}, u32[]{:S(2)}) copy-start(f32[3,256]{1,0:T(4,128)} %copy-done.47) | copy-start | bytes 9220
  427.2 67.6 %copy-start.56 = (f32[768]{0:T(1024)S(1)}, f32[768]{0:T(1024)}, u32[]{:S(2)}) copy-start(f32[768]{0:T(1024)} %param.33) | copy-start | bytes 9220
  558.6 144.9 %all-reduce.19.cloned.1.call-start = ((), (), s32[]{:S(2)}) async-start(), calls=%async_computation.15 | async-start | bytes 4718592 | tf_op jit(solution)/shard_map/psum | solution.py:224
  558.6 13.7 %slice-start = ((s8[4718592]{0:T(1024)(128)(4,1)}), s8[524288]{0:T(1024)(128)(4,1)S(1)}, s32[]{:S(2)}) async-start(s8[4718592]{0:T(1024)(128)(4,1)} %bitcast.364), calls=%async_computation.16 | async-start | bytes 1048576
  563.8 8.4 slice-start.1
  569.3 58.4 %collective-permute-start.2 = (bf16[3,256,2,384]{3,1,2,0:T(8,128)(2,1)}, bf16[3,256,2,384]{3,1,2,0:T(8,128)(2,1)}, u32[]{:S(2)}, u32[]{:S(2)}) collective-permute-start(bf16[3,256,2,384]{3,1,2,0:T(8,128)(2,1)} %get-tuple-element.219), channel_id=1, source_target_pairs={{4,0},{6,2},{5,1},{7,3},{12,8},{14,10},{13,9},{15,11},{20,16},{22,... | collective-permute-start | bytes 3538952 | tf_op jit(solution)/shard_map/ppermute | solution.py:19
  570.6 57.0 %collective-permute-start.3 = (bf16[3,256,2,384]{3,1,2,0:T(8,128)(2,1)}, bf16[3,256,2,384]{3,1,2,0:T(8,128)(2,1)}, u32[]{:S(2)}, u32[]{:S(2)}) collective-permute-start(bf16[3,256,2,384]{3,1,2,0:T(8,128)(2,1)} %get-tuple-element.220), channel_id=1, source_target_pairs={{2,0},{4,2},{6,4},{3,1},{5,3},{7,5},{10,8},{12,10},{14,12},{11,9},... | collective-permute-start | bytes 3538952 | tf_op jit(solution)/shard_map/ppermute | solution.py:19
  576.4 31.2 %copy-start.26 = (bf16[128,512]{1,0:T(8,128)(2,1)S(1)}, bf16[128,512]{1,0:T(8,128)(2,1)}, u32[]{:S(2)}) copy-start(bf16[128,512]{1,0:T(8,128)(2,1)} %copy-done.25) | copy-start | bytes 393220
  576.4 31.2 %copy-start.28 = (bf16[128,512]{1,0:T(8,128)(2,1)S(1)}, bf16[128,512]{1,0:T(8,128)(2,1)}, u32[]{:S(2)}) copy-start(bf16[128,512]{1,0:T(8,128)(2,1)} %copy-done.27) | copy-start | bytes 393220
  634.5 93.9 %reduce-scatter.7.cloned.1.call-start = ((), (), s32[]{:S(2)}) async-start(), calls=%async_computation.11 | async-start | bytes 737280 | tf_op jit(solution)/shard_map/reduce_scatter | solution.py:348
  637.8 139.5 %reduce-scatter.9.cloned.1.call-start = ((), (), s32[]{:S(2)}) async-start(), calls=%async_computation.12 | async-start | bytes 2949120 | tf_op jit(solution)/shard_map/reduce_scatter | solution.py:351
  643.6 183.5 %reduce-scatter.11.cloned.1.call-start = ((), (), s32[]{:S(2)}) async-start(), calls=%async_computation.13 | async-start | bytes 2949120 | tf_op jit(solution)/shard_map/reduce_scatter | solution.py:354
  650.8 216.7 %reduce-scatter.5.cloned.1.call-start = ((), (), s32[]{:S(2)}) async-start(), calls=%async_computation.10 | async-start | bytes 2211840 | tf_op jit(solution)/shard_map/reduce_scatter | solution.py:345
  656.2 280.4 %all-reduce.17.cloned.1.call-start = ((), (), s32[]{:S(2)}) async-start(), calls=%async_computation.14 | async-start | bytes 3538944 | tf_op jit(solution)/shard_map/psum | solution.py:359
  936.5 5.9 copy-start.22
  (65 other events, 209.3 us)
Sparse Core Ops, SparseCore 0:
  9.6 43.0 all-gather.3
  235.8 71.0 all-reduce.10
  308.6 50.4 all-gather.5
  360.6 49.2 all-gather.7
  423.4 67.4 all-reduce.12
  558.7 48.8 all-reduce.14
  634.6 68.7 all-reduce.18
  706.4 21.9 reduce-scatter.6
  730.8 46.4 reduce-scatter.8
  779.5 47.5 reduce-scatter.10
  829.5 37.8 reduce-scatter.4
  869.9 46.5 all-reduce.16
where the time goes:
time: 962 us; the launch traced here: 951 us
  waiting for transfers between devices  449 us (47%)
  matrix products  140 us (15%)
  blocking collectives  125 us (13%)
  other arithmetic  124 us (13%)
  local copies, waits for them, and re-layouts  84.5 us (9%)
  between operations  17.1 us (2%)
  starting transfers between devices  10.6 us (1%)
    psum x1, waiting for transfers between devices, per_device(): attn_sum = lax.psum(attn_part, 'tp')  69.9 us
    psum x1, waiting for transfers between devices, per_device(): grad_mlp_normed = lax.psum(mlp_back_part, 'tp')  63.6 us
    psum x1, blocking collectives, per_device(): lax.psum((attn_gain_grad, attn_shift_grad, qkv_bias_grad, center_grad, sp...  61.4 us
    reduce_scatter x1, waiting for transfers between devices, per_device(): lax.psum_scatter(proj_grad.astype(jnp.bfloat16), 'dp', scatter_dimension=...  49.8 us
    reduce_scatter x1, waiting for transfers between devices, per_device(): lax.psum_scatter(fc_grad.astype(jnp.bfloat16), 'dp', scatter_dimension=0,...  48.9 us
    all_gather x1, waiting for transfers between devices, per_device(): lax.all_gather(fc_weight, 'dp', axis=0, tiled=True)  47.6 us
    psum x1, blocking collectives, per_device(): memory = lax.psum(partial_memory, 'ctx').astype(jnp.bfloat16)  45 us
    all_gather x1, waiting for transfers between devices, per_device(): lax.all_gather(proj_weight, 'dp', axis=1, tiled=True)  44.1 us
  transfers between devices with their start and end apart: 16, of which 10 were waited for; matrix products, arithmetic and copies ran while one was open for 21% of the time, Pallas kernels for 0%

commit v1 on v0

v1 whole, which is shorter than its diff:
```python
import functools

import jax
import jax.numpy as jnp
import numpy as np
from jax import lax
from jax.experimental import pallas as pl
from jax.experimental.pallas import tpu as pltpu
from jax.sharding import PartitionSpec as P

DH = 64
WINDOW = 512
EPS = 1e-05
SPREAD = 0.02
SCALE = DH ** (-0.5)
VMEM_LIMIT = 58 * 1024 * 1024

bf16 = jnp.bfloat16
f32 = jnp.float32
MESH = pl.DeviceIdType.MESH


def dot_nn(a, b):
    return lax.dot_general(a, b, (((1,), (0,)), ((), ())), preferred_element_type=f32)


def dot_nt(a, b):
    return lax.dot_general(a, b, (((1,), (1,)), ((), ())), preferred_element_type=f32)


def dot_tn(a, b):
    return lax.dot_general(a, b, (((0,), (0,)), ((), ())), preferred_element_type=f32)


def ridge_fit(basis_count, sample_count):
    centers = (np.arange(basis_count) + 0.5) / basis_count
    times = (np.arange(sample_count) + 0.5) / sample_count
    width = 1.0 / basis_count
    design = np.exp(-np.square(times[None, :] - centers[:, None]) / (2.0 * width * width))
    gram = design @ design.T + 0.5 * np.eye(basis_count)
    return np.linalg.solve(gram, design).astype(bf16)


def place():
    c = lax.axis_index("ctx")
    side = c + 1 - 2 * lax.rem(c, 2)
    across = lax.rem(c + 2, 4)
    corner = lax.rem(side + 2, 4)
    return lax.axis_index("dp"), c, lax.axis_index("tp"), side, across, corner


def enter(devices):
    barrier = pltpu.get_barrier_semaphore()
    for device in devices:
        pl.semaphore_signal(barrier, inc=1, device_id=device, device_id_type=MESH)
    pl.semaphore_wait(barrier, len(devices))


def remote(src, dst, send, recv, device):
    return pltpu.make_async_remote_copy(
        src_ref=src,
        dst_ref=dst,
        send_sem=send,
        recv_sem=recv,
        device_id=device,
        device_id_type=MESH,
    )


def normalise(x, gain, shift):
    mean = jnp.mean(x, axis=-1, keepdims=True)
    centred = x - mean
    r = lax.rsqrt(jnp.mean(centred * centred, axis=-1, keepdims=True) + EPS)
    n = centred * r
    return n * gain + shift, n, r


def lowest_key(lengths, s, pos):
    low = jnp.maximum(pos - (WINDOW - 1), 0)
    end = jnp.int32(0)
    for e in range(lengths.shape[1]):
        end = end + lengths[s, e]
        low = jnp.maximum(low, jnp.where(pos >= end, end, 0))
    return low


def lanes(shape, dim):
    return lax.broadcasted_iota(jnp.int32, shape, dim)


def half_lanes(scale):
    lane = lanes((1, 2 * DH), 1)
    return [
        jnp.where(lane < DH, scale, 0.0).astype(bf16),
        jnp.where(lane >= DH, scale, 0.0).astype(bf16),
    ]


def mask_bias(lengths, s, c, rows, key_start, keys):
    pos = c * rows + lanes((rows, 1), 0)
    low = lowest_key(lengths, s, pos)
    key_pos = key_start + lanes((1, keys), 1)
    return jnp.where((key_pos <= pos) & (key_pos >= low), 0.0, -1e30)


def reach_terms(scores, center_row, spread_row, centers, width):
    center_logit = jnp.sum(scores * center_row, axis=-1, keepdims=True)
    spread_logit = jnp.sum(scores * spread_row, axis=-1, keepdims=True)
    mu = 1.0 / (1.0 + jnp.exp(-center_logit))
    grown = jnp.exp(spread_logit)
    var = SPREAD * jnp.log(1.0 + grown) + width * width
    inv = 1.0 / var
    diff = mu - centers
    reach = (width * lax.rsqrt(var)) * jnp.exp(-(diff * diff) * (0.5 * inv))
    return reach, mu, inv, diff, spread_logit


def forward_kernel(gather, refs):
    n = lax.axis_size("dp")
    if gather:
        (hid, lengths, places, gain, shift, wq_sh, wo_sh, wf_sh, wp_sh, qbias, cw, sw, fit,
         normed, q, kv, mem, lse, mixed, wq, wo, wf, wp,
         hoth, noth, bias, lsem,
         zs, zr, ys, yr, as_, ar, bs, br, os_, or_, hys, hyr, hxs, hxr, ks, kr, ms, mr) = refs
    else:
        (hid, lengths, places, gain, shift, wq, qbias, cw, sw, fit,
         normed, q, kv, mem, lse, mixed,
         hoth, noth, bias,
         hys, hyr, hxs, hxr, ks, kr, ms, mr) = refs
    z, c, t, side, across, corner = place()
    S, B, D = hid.shape
    HW = q.shape[2]
    NB = mem.shape[1]
    L = kv.shape[1]
    half = B // 2
    peers = [{"ctx": side}, {"ctx": across}, {"tp": 1 - t}]
    if gather:
        R = D // n
        Q = R // 4
        shards = [wq_sh, wo_sh, wf_sh, wp_sh]
        whole = [wq, wo.at[t], wf, wp]
        peers += [{"dp": lax.rem(z + i, n)} for i in range(1, n)]
    enter(peers)

    started = []

    def start(copies):
        for copy in copies:
            copy.start()
        started.extend(copies)
        return copies

    if gather:

        def rows(g, owner, quarter):
            return whole[g].at[pl.ds(pl.multiple_of(R * owner + Q * quarter, 16), Q)]

        def source(i):
            return lax.rem(z + n - i, n)

        def z_copies(g):
            src = shards[g].at[pl.ds(pl.multiple_of(Q * c, 16), Q)]
            return [
                remote(src, rows(g, z, c), zs.at[g, i - 1], zr.at[g, i - 1], {"dp": lax.rem(z + i, n)})
                for i in range(1, n)
            ]

        def own_copy(g):
            return pltpu.make_async_copy(
                shards[g], whole[g].at[pl.ds(pl.multiple_of(R * z, 16), R)], lsem.at[g]
            )

        def y_copies(g):
            return [
                remote(rows(g, source(i), c), rows(g, source(i), c), ys.at[g, i - 1], yr.at[g, i - 1], {"ctx": across})
                for i in range(1, n)
            ]

        def a_copies(g):
            return [
                remote(rows(g, source(i), c), rows(g, source(i), c), as_.at[g, i - 1], ar.at[g, i - 1], {"ctx": side})
                for i in range(1, n)
            ]

        def b_copies(g):
            return [
                remote(rows(g, source(i), across), rows(g, source(i), across), bs.at[g, i - 1], br.at[g, i - 1], {"ctx": side})
                for i in range(1, n)
            ]

        z_sent, y_sent, a_sent, b_sent, own_sent = {}, {}, {}, {}, {}

        def stage_z(g):
            own_sent[g] = own_copy(g)
            own_sent[g].start()
            z_sent[g] = start(z_copies(g))

        def stage_y(g):
            for copy in z_sent[g]:
                copy.wait_recv()
            y_sent[g] = start(y_copies(g))
            a_sent[g] = start(a_copies(g))

        def stage_b(g):
            for copy in y_sent[g]:
                copy.wait_recv()
            b_sent[g] = start(b_copies(g))

        def stage_end(g):
            for copy in a_sent[g] + b_sent[g]:
                copy.wait_recv()
            own_sent[g].wait()
    else:

        def stage_z(g):
            pass

        stage_y = stage_b = stage_end = stage_z

    def hidden_y(s):
        piece = pl.ds(pl.multiple_of(half * t, 16), half)
        return remote(hid.at[s, piece], hoth.at[s, piece], hys.at[s], hyr.at[s], {"ctx": across})

    def hidden_x(s):
        piece = pl.ds(pl.multiple_of(half * t, 16), half)
        return remote(hoth.at[s, piece], hoth.at[s, piece], hxs.at[s], hxr.at[s], {"tp": 1 - t})

    def block(s, owner):
        return kv.at[s, pl.ds(pl.multiple_of(owner * B, B), B)]

    def kv_copy(s, which):
        owner = c if which == 0 else across
        return remote(block(s, owner), block(s, owner), ks.at[s, which], kr.at[s, which], {"ctx": side})

    stage_z(0)
    hy = start([hidden_y(s) for s in range(S)])
    for g in (1, 2, 3):
        stage_z(g)

    gain_row = gain[...]
    shift_row = shift[...]
    for s in range(S):
        low, _, _ = normalise(hid[s].astype(f32), gain_row, shift_row)
        normed[s] = low.astype(bf16)
    hx = []
    for s in range(S):
        hy[s].wait_recv()
        hx += start([hidden_x(s)])
    stage_y(0)
    for s in range(S):
        hx[s].wait_recv()
        low, _, _ = normalise(hoth[s].astype(f32), gain_row, shift_row)
        noth[s] = low.astype(bf16)
    stage_b(0)
    stage_end(0)
    bias_row = qbias[...]
    kvs = []
    for s in range(S):
        part = (dot_nn(normed[s], wq[:, HW:]) + bias_row[:, HW:]).astype(bf16)
        kv[s, pl.ds(pl.multiple_of(c * B, B), B)] = part
        kvs += start([kv_copy(s, 0)])
    stage_y(1)
    for s in range(S):
        part = (dot_nn(noth[s], wq[:, HW:]) + bias_row[:, HW:]).astype(bf16)
        kv[s, pl.ds(pl.multiple_of(across * B, B), B)] = part
        kvs += start([kv_copy(s, 1)])
    stage_b(1)
    stage_y(2)
    for s in range(S):
        q[s] = (dot_nn(normed[s], wq[:, :HW]) + bias_row[:, :HW]).astype(bf16)
    stage_end(1)
    if gather:
        wo_sent = start([remote(wo.at[t], wo.at[t], os_, or_, {"tp": 1 - t})])

    key_start = pl.multiple_of(jnp.maximum(c - 2, 0) * B, B)
    keys = 3 * B
    M = places.shape[0]
    centers = (lanes((1, NB), 1).astype(f32) + 0.5) * (1.0 / NB)
    width = 1.0 / NB
    lane = lanes((1, 2 * DH), 1)
    scaled = half_lanes(SCALE)
    column = lanes((1, 2 * DH), 1)
    mx = []
    for s in range(S):
        kvs[s].wait_recv()
        kvs[S + s].wait_recv()
        key_row = lanes((1, L), 1)
        sticky = jnp.where(key_row == places[:, s : s + 1], 1.0, 0.0).astype(bf16)
        even = lanes((M, 1), 0) * L // M + L // (2 * M)
        steady = jnp.where(key_row == even, 1.0, 0.0).astype(bf16)
        spread_fit = dot_nn(fit[:, :M], sticky) + dot_nn(fit[:, M:], steady)
        high = spread_fit.astype(bf16)
        rest = (spread_fit - high.astype(f32)).astype(bf16)
        mem[s] = (dot_nn(high, kv[s]) + dot_nn(rest, kv[s])).astype(bf16)
        bias[...] = mask_bias(lengths, s, c, B, key_start, keys)

        def pair_step(p, log_rows, s=s):
            cols = pl.ds(pl.multiple_of(p * 2 * DH, 2 * DH), 2 * DH)
            vcols = pl.ds(pl.multiple_of(HW + p * 2 * DH, 2 * DH), 2 * DH)
            window = pl.ds(key_start, keys)
            qp = q[s, :, cols]
            kp = kv[s, window, cols]
            vp = kv[s, window, vcols]
            mk = mem[s, :, cols]
            mv = mem[s, :, vcols]
            outs = []
            for h in range(2):
                qh = qp * scaled[h]
                scores = dot_nt(qh, kp) + bias[...]
                top = jnp.max(scores, axis=-1, keepdims=True)
                e = jnp.exp(scores - top)
                total = jnp.sum(e, axis=-1, keepdims=True)
                share = (e * (1.0 / total)).astype(bf16)
                out = dot_nn(share, vp)
                log_rows = jnp.where(column == 2 * p + h, top + jnp.log(total), log_rows)
                mem_scores = dot_nt(qh, mk)
                reach, _, _, _, _ = reach_terms(
                    mem_scores, cw[pl.ds(2 * p + h, 1)], sw[pl.ds(2 * p + h, 1)], centers, width
                )
                outs.append(out + dot_nn(reach.astype(bf16), mv))
            mixed[t, s, :, cols] = jnp.where(lane < DH, outs[0], outs[1]).astype(bf16)
            return log_rows

        lse[s] = lax.fori_loop(0, HW // (2 * DH), pair_step, jnp.zeros((B, 2 * DH), f32))
        mx += start([remote(mixed.at[t, s], mixed.at[t, s], ms.at[s], mr.at[s], {"tp": 1 - t})])
        if s == 0:
            stage_b(2)
            stage_y(3)
        if s == 1:
            stage_b(3)
    stage_end(2)
    stage_end(3)
    if gather:
        wo_sent[0].wait_recv()
    for copy in mx:
        copy.wait_recv()
    for copy in started:
        copy.wait_send()


def forward(gather, hid, lengths, places, gain, shift, weights, qbias, cw, sw, fit):
    S, B, D = hid.shape
    HW = qbias.shape[1] // 3
    n = lax.axis_size("dp")
    L = B * lax.axis_size("ctx")
    NB = cw.shape[1]
    vm = pl.BlockSpec(memory_space=pltpu.VMEM)
    sm = pl.BlockSpec(memory_space=pltpu.SMEM)
    hb = pl.BlockSpec(memory_space=pl.ANY)
    out = [
        jax.ShapeDtypeStruct((S, B, D), bf16),
        jax.ShapeDtypeStruct((S, B, HW), bf16),
        jax.ShapeDtypeStruct((S, L, 2 * HW), bf16),
        jax.ShapeDtypeStruct((S, NB, 2 * HW), bf16),
        jax.ShapeDtypeStruct((S, B, 128), f32),
        jax.ShapeDtypeStruct((2, S, B, HW), bf16),
    ]
    out_specs = [vm] * 6
    sem = pltpu.SemaphoreType.DMA
    scratch = [
        pltpu.VMEM((S, B, D), bf16),
        pltpu.VMEM((S, B, D), bf16),
        pltpu.VMEM((B, 3 * B), f32),
    ]
    w_specs = [vm]
    if gather:
        FW = weights[2].shape[1]
        out += [
            jax.ShapeDtypeStruct((D, 3 * HW), bf16),
            jax.ShapeDtypeStruct((2, D, HW), bf16),
            jax.ShapeDtypeStruct((D, FW), bf16),
            jax.ShapeDtypeStruct((D, FW), bf16),
        ]
        out_specs += [vm, hb, hb, hb]
        w_specs = [vm, hb, hb, hb]
        scratch += [sem((4,))] + [sem((4, n - 1))] * 8 + [sem, sem]
    scratch += [sem((S,))] * 4 + [sem((S, 2))] * 2 + [sem((S,))] * 2
    return pl.pallas_call(
        lambda *refs: forward_kernel(gather, refs),
        out_shape=out,
        in_specs=[vm, sm, vm, vm, vm, *w_specs, vm, vm, vm, vm],
        out_specs=out_specs,
        scratch_shapes=scratch,
        compiler_params=pltpu.CompilerParams(
            collective_id=0, has_side_effects=True, vmem_limit_bytes=VMEM_LIMIT
        ),
        cost_estimate=pl.CostEstimate(flops=6_000_000_000, bytes_accessed=30_000_000, transcendentals=6_000_000),
        name="forward_part",
    )(hid, lengths, places, gain, shift, *weights, qbias, cw, sw, fit)


def layer_norm(values, gain_vec, shift_vec):
    mean_value = jnp.mean(values, axis=-1, keepdims=True)
    centred = values - mean_value
    variance = jnp.mean(centred * centred, axis=-1, keepdims=True)
    return centred * lax.rsqrt(variance + EPS) * gain_vec + shift_vec


def gelu_tanh(values):
    return (
        0.5
        * values
        * (1.0 + jnp.tanh(0.7978845608028654 * (values + 0.044715 * values * values * values)))
    )


def memory_reach(mem_scores, center_weight, spread_weight):
    highest = lax.Precision.HIGHEST
    basis_count = mem_scores.shape[-1]
    centers = (jnp.arange(basis_count, dtype=f32) + 0.5) / basis_count
    basis_width = 1.0 / basis_count
    center_logit = jnp.einsum("...hqj,hj->...hq", mem_scores, center_weight, precision=highest)
    spread_logit = jnp.einsum("...hqj,hj->...hq", mem_scores, spread_weight, precision=highest)
    middle = jax.nn.sigmoid(center_logit)[..., None]
    variance = (SPREAD * jnp.log1p(jnp.exp(spread_logit)) + basis_width * basis_width)[..., None]
    return basis_width * lax.rsqrt(variance) * jnp.exp(-jnp.square(middle - centers) / (2.0 * variance))


def attend_back(item):
    queries, key_rows, value_rows, bias, log_total, grad_mixed = item
    masked = jnp.einsum("qhd,khd->hqk", queries, key_rows, preferred_element_type=f32) * SCALE + bias[None]
    shares = jnp.exp(masked - log_total)
    grad_shares = jnp.einsum("qhd,khd->hqk", grad_mixed, value_rows, preferred_element_type=f32)
    grad_scores = (shares * (grad_shares - jnp.sum(shares * grad_shares, axis=-1, keepdims=True))).astype(bf16)
    grad_queries = jnp.einsum("hqk,khd->qhd", grad_scores, key_rows, preferred_element_type=f32) * SCALE
    grad_keys = jnp.einsum("hqk,qhd->khd", grad_scores, queries, preferred_element_type=f32) * SCALE
    grad_values = jnp.einsum("hqk,qhd->khd", shares.astype(bf16), grad_mixed, preferred_element_type=f32)
    return (grad_queries, grad_keys, grad_values)


def passed_along(value, axis, distance):
    devices = range(lax.axis_size(axis))
    return lax.ppermute(value, axis, [(i - distance, i) for i in devices if i - distance in devices])


def per_device(hidden_in, doc_lengths, sticky_places, attn_gain, attn_shift, qkv_weight, qkv_bias, center_weight,
               spread_weight, out_weight, out_bias, mlp_gain, mlp_shift, fc_weight, fc_bias, proj_weight, proj_bias, cotangent):
    S, B, D = hidden_in.shape
    n = lax.axis_size("dp")
    HW = qkv_bias.shape[1]
    H = HW // DH
    NB = center_weight.shape[1]
    c = lax.axis_index("ctx")
    t = lax.axis_index("tp")
    M = sticky_places.shape[1]
    L = B * lax.axis_size("ctx")
    fit = jnp.asarray(ridge_fit(NB, 2 * M))
    gather = D % (64 * n) == 0
    shards = [qkv_weight.reshape(D // n, 3 * HW), out_weight.T, fc_weight, proj_weight.T]
    if gather:
        weights = shards
    else:
        full = [lax.all_gather(w, "dp", axis=0, tiled=True) for w in shards]
        weights = full[:1]
    res = forward(gather, hidden_in, doc_lengths, sticky_places.T, attn_gain[None], attn_shift[None], weights,
                  qkv_bias.reshape(1, 3 * HW), center_weight, spread_weight, fit)
    normed_low, q, kv, memory, lse, mixed = res[:6]
    if gather:
        wq, wo, wf, wp = res[6:]
        wo = lax.dynamic_index_in_dim(wo, t, 0, keepdims=False)
    else:
        wq, wo, wf, wp = full
    qkv_full, out_full, fc_full, proj_full = wq.reshape(D, 3, HW), wo.T, wf, wp.T
    inputs_wide = hidden_in.astype(f32)
    _, norm_pull = jax.vjp(layer_norm, inputs_wide, attn_gain, attn_shift)
    queries = q.reshape(S, B, H, DH)
    key_start = jnp.maximum(c - 2, 0) * B
    win = lax.dynamic_slice_in_dim(kv, key_start, 3 * B, axis=1)
    key_rows = win[:, :, :HW].reshape(S, 3 * B, H, DH)
    value_rows = win[:, :, HW:].reshape(S, 3 * B, H, DH)
    pos = c * B + jnp.arange(B)
    kpos = key_start + jnp.arange(3 * B)
    ends = jnp.sum(jnp.where(jnp.tril(jnp.ones((doc_lengths.shape[1],) * 2, bool))[None], doc_lengths[:, None, :], 0), axis=2)
    qd = jnp.sum((ends[:, None, :] <= pos[None, :, None]).astype(jnp.int32), axis=2)
    kd = jnp.sum((ends[:, None, :] <= kpos[None, :, None]).astype(jnp.int32), axis=2)
    allowed = (kpos[None, None, :] <= pos[None, :, None]) & (pos[None, :, None] - kpos[None, None, :] < WINDOW) & (qd[:, :, None] == kd[:, None, :])
    bias = jnp.where(allowed, 0.0, -1e30)
    mem_keys = memory[:, :, :HW].reshape(S, NB, H, DH)
    mem_values = memory[:, :, HW:].reshape(S, NB, H, DH)
    mem_scores = jnp.einsum("sqhd,sbhd->shqb", queries, mem_keys, preferred_element_type=f32) * SCALE
    reach_weights, reach_pull = jax.vjp(memory_reach, mem_scores, center_weight, spread_weight)
    reach_low = reach_weights.astype(bf16)
    mixed_heads = lax.dynamic_index_in_dim(mixed, t, 0, keepdims=False)
    attn_part = jnp.einsum("sbe,ed->sbd", mixed_heads, out_full, preferred_element_type=f32)
    residual = inputs_wide + lax.psum(attn_part, "tp") + out_bias
    mlp_normed, mlp_pull = jax.vjp(layer_norm, residual, mlp_gain, mlp_shift)
    mlp_low = mlp_normed.astype(bf16)
    pre_act = jnp.einsum("sbd,df->sbf", mlp_low, fc_full, preferred_element_type=f32) + fc_bias
    activated, gelu_pull = jax.vjp(gelu_tanh, pre_act)
    activated_low = activated.astype(bf16)
    mlp_part = jnp.einsum("sbf,fd->sbd", activated_low, proj_full, preferred_element_type=f32)
    mlp_sum = lax.psum(mlp_part.astype(bf16), "tp").astype(f32)
    block_out = (residual + mlp_sum + proj_bias).astype(bf16)
    grad_out = cotangent.astype(f32)
    proj_grad = jnp.einsum("sbf,sbd->fd", activated_low, cotangent, preferred_element_type=f32)
    proj_bias_grad = jnp.sum(grad_out, axis=(0, 1))
    grad_activated = jnp.einsum("sbd,fd->sbf", cotangent, proj_full, preferred_element_type=f32)
    grad_pre = gelu_pull(grad_activated)[0].astype(bf16)
    fc_grad = jnp.einsum("sbd,sbf->df", mlp_low, grad_pre, preferred_element_type=f32)
    fc_bias_grad = jnp.sum(grad_pre, axis=(0, 1), dtype=f32)
    mlp_back_part = jnp.einsum("sbf,df->sbd", grad_pre, fc_full, preferred_element_type=f32)
    grad_mlp_normed = lax.psum(mlp_back_part, "tp")
    grad_residual, mlp_gain_grad, mlp_shift_grad = mlp_pull(grad_mlp_normed)
    grad_residual = grad_residual + grad_out
    out_bias_grad = jnp.sum(grad_residual, axis=(0, 1))
    grad_residual_low = grad_residual.astype(bf16)
    out_grad = jnp.einsum("sbe,sbd->ed", mixed_heads, grad_residual_low, preferred_element_type=f32)
    grad_mixed = jnp.einsum("sbd,ed->sbe", grad_residual_low, out_full, preferred_element_type=f32)
    grad_mixed = grad_mixed.astype(bf16).reshape(S, B, H, DH)
    log_total = jnp.swapaxes(lse[:, :, :H], 1, 2)[..., None]
    grad_queries, grad_keys, grad_values = lax.map(attend_back, (queries, key_rows, value_rows, bias, log_total, grad_mixed))
    grad_reach = jnp.einsum("sqhd,sbhd->shqb", grad_mixed, mem_values, preferred_element_type=f32)
    grad_mem_values = jnp.einsum("shqb,sqhd->sbhd", reach_low, grad_mixed, preferred_element_type=f32)
    grad_mem_scores, center_grad, spread_grad = reach_pull(grad_reach)
    grad_mem_scores = grad_mem_scores.astype(bf16)
    grad_queries = grad_queries + jnp.einsum("shqb,sbhd->sqhd", grad_mem_scores, mem_keys, preferred_element_type=f32) * SCALE
    grad_mem_keys = jnp.einsum("shqb,sqhd->sbhd", grad_mem_scores, queries, preferred_element_type=f32) * SCALE
    grad_memory_part = jnp.concatenate([grad_mem_keys.reshape(S, NB, HW), grad_mem_values.reshape(S, NB, HW)], axis=2)
    grad_memory = lax.psum(grad_memory_part.astype(bf16), "ctx")
    grad_sampled = jnp.einsum("bm,sbc->smc", fit, grad_memory, preferred_element_type=f32)
    uniform = jnp.arange(M, dtype=jnp.int32) * L // M + L // (2 * M)
    all_places = jnp.concatenate([sticky_places, jnp.broadcast_to(uniform, sticky_places.shape)], axis=1)
    local_index = all_places - c * B
    inside = (local_index >= 0) & (local_index < B)
    row_index = jnp.where(inside, local_index, B)
    seq_index = jnp.arange(S, dtype=jnp.int32)[:, None]
    grad_fit_rows = jnp.zeros((S, B, 2 * HW), f32).at[seq_index, row_index].add(grad_sampled, mode="drop")
    grad_win = jnp.concatenate([grad_keys.reshape(S, 3 * B, HW), grad_values.reshape(S, 3 * B, HW)], axis=2)
    grad_all = lax.dynamic_update_slice_in_dim(jnp.zeros((S, L, 2 * HW), f32), grad_win, key_start, axis=1)
    grad_own = lax.psum_scatter(grad_all, "ctx", scatter_dimension=1, tiled=True) + grad_fit_rows
    grad_qkv = jnp.concatenate([grad_queries.reshape(S, B, 1, HW), grad_own.reshape(S, B, 2, HW)], axis=2).astype(bf16)
    qkv_grad = jnp.einsum("sbd,sbke->dke", normed_low, grad_qkv, preferred_element_type=f32)
    qkv_bias_grad = jnp.sum(grad_qkv, axis=(0, 1), dtype=f32)
    grad_normed = lax.psum(jnp.einsum("sbke,dke->sbd", grad_qkv, qkv_full, preferred_element_type=f32).astype(bf16), "tp").astype(f32)
    grad_inputs, attn_gain_grad, attn_shift_grad = norm_pull(grad_normed)
    input_grad = (grad_inputs + grad_residual).astype(bf16)
    small = lax.psum((attn_gain_grad, attn_shift_grad, qkv_bias_grad, center_grad, spread_grad, out_bias_grad, mlp_gain_grad, mlp_shift_grad, fc_bias_grad, proj_bias_grad), ("dp", "ctx"))
    attn_gain_grad, attn_shift_grad, qkv_bias_grad, center_grad, spread_grad, out_bias_grad, mlp_gain_grad, mlp_shift_grad, fc_bias_grad, proj_bias_grad = small

    def reduced(grad, dim):
        part = lax.psum_scatter(grad.astype(bf16), "dp", scatter_dimension=dim, tiled=True)
        return lax.psum(part, "ctx").astype(f32)

    return (block_out, input_grad, attn_gain_grad, attn_shift_grad, reduced(qkv_grad, 0), qkv_bias_grad, center_grad, spread_grad,
            reduced(out_grad, 1), out_bias_grad, mlp_gain_grad, mlp_shift_grad, reduced(fc_grad, 0), fc_bias_grad, reduced(proj_grad, 1), proj_bias_grad)


def solution(mesh):
    in_specs = (
        P("dp", "ctx", None),
        P("dp", None),
        P("dp", None),
        P(),
        P(),
        P("dp", None, "tp"),
        P(None, "tp"),
        P("tp", None),
        P("tp", None),
        P("tp", "dp"),
        P(),
        P(),
        P(),
        P("dp", "tp"),
        P("tp"),
        P("tp", "dp"),
        P(),
        P("dp", "ctx", None),
    )
    out_specs = (
        P("dp", "ctx", None),
        P("dp", "ctx", None),
        P(),
        P(),
        P("dp", None, "tp"),
        P(None, "tp"),
        P("tp", None),
        P("tp", None),
        P("tp", "dp"),
        P(),
        P(),
        P(),
        P("dp", "tp"),
        P("tp"),
        P("tp", "dp"),
        P(),
    )
    return jax.shard_map(
        per_device, mesh=mesh, in_specs=in_specs, out_specs=out_specs, check_vma=False
    )
```

time: 962 us -> 774 us (0.80)
  waiting for transfers between devices: 449 us -> 362 us
  Pallas kernels: 0 us -> 75.3 us
  blocking collectives: 125 us -> 61.4 us
  other arithmetic: 124 us -> 63.8 us
  matrix products: 140 us -> 115 us
  local copies, waits for them, and re-layouts: 84.5 us -> 69.3 us
    all_gather x3 -> x0, waiting for transfers between devices: 91.8 us -> none  [the longest x1 47.6 us: per_device(): lax.all_gather(fc_weight, 'dp', axis=0, tiled=True)]
    pallas_call x0 -> x1, Pallas kernels: none -> 75.3 us  [forward(): pl.pallas_call(lambda *refs: forward_kernel(gather, refs), out_shape=out,...]
    another operation x14 -> x3, other arithmetic: 61.3 us -> 1.78 us  [the longest x6 34 us: ridge_fit(): factor = jnp.linalg.cholesky(gram_matrix)]
    reduce_scatter x4 -> x5, waiting for transfers between devices: 158 us -> 217 us  [the longest x4 159 us: reduced(): lax.psum_scatter(grad.astype(bf16), 'dp', scatter_dimension=dim, tiled=True)]
    psum x1 -> x0, blocking collectives: 45 us -> none  [per_device(): memory = lax.psum(partial_memory, 'ctx').astype(jnp.bfloat16)]
    psum x4, waiting for transfers between devices: 133 us -> 90.5 us  [the longest x1 56.8 us: per_device(): residual = inputs_wide + lax.psum(attn_part, 'tp') + out_bias]
    dot_general x27 -> x17, matrix products: 73.4 us -> 46.5 us  [the longest x1 6.56 us: per_device(): jnp.einsum('sbd,fd->sbf', cotangent, proj_full, preferred_element_type=f32)]
    gather x3 -> x0, local copies, waits for them, and re-layouts: 25 us -> none  [per_device(): jnp.take_along_axis(kv_flat, jnp.clip(local_index, 0, block_rows - 1)[:,...]
  transfers between devices with their start and end apart: 16 -> 10, of which waited for: 10 -> 8; matrix products, arithmetic and copies ran while one was open for 21% -> 21% of each run, Pallas kernels for 0% -> 0%
where the time goes in v1:
time: 774 us; the launch traced here: 763 us
  waiting for transfers between devices  362 us (47%)
  matrix products  115 us (15%)
  Pallas kernels  75.3 us (10%)
  local copies, waits for them, and re-layouts  69.3 us (9%)
  other arithmetic  63.8 us (8%)
  blocking collectives  61.4 us (8%)
  between operations  15.3 us (2%)
    reduce_scatter x4, waiting for transfers between devices, reduced(): lax.psum_scatter(grad.astype(bf16), 'dp', scatter_dimension=dim, tiled=True)  159 us
    pallas_call x1, Pallas kernels, forward(): pl.pallas_call(lambda *refs: forward_kernel(gather, refs), out_shape=out,...  75.3 us
    psum x1, blocking collectives, per_device(): lax.psum((attn_gain_grad, attn_shift_grad, qkv_bias_grad, center_grad, sp...  61.4 us
    reduce_scatter x1, waiting for transfers between devices, per_device(): lax.psum_scatter(grad_all, 'ctx', scatter_dimension=1, tiled=True)  57.8 us
    psum x1, waiting for transfers between devices, per_device(): residual = inputs_wide + lax.psum(attn_part, 'tp') + out_bias  56.8 us
    psum x1, waiting for transfers between devices, per_device(): grad_mlp_normed = lax.psum(mlp_back_part, 'tp')  54.4 us
    psum x1, waiting for transfers between devices, per_device(): mlp_sum = lax.psum(mlp_part.astype(bf16), 'tp').astype(f32)  33.6 us
  transfers between devices with their start and end apart: 10, of which 8 were waited for; matrix products, arithmetic and copies ran while one was open for 21% of the time, Pallas kernels for 0%

profile of v1, /device:TPU:0, one launch (start us, length us, event | category | flops | bytes accessed | tf_op | source)
XLA Modules:
  0.0 763.5 jit_solution(104664228568136427)
XLA Ops:
  14.4 75.3 %forward_part.1 = (bf16[3,256,768]{2,1,0:T(8,128)(2,1)}, bf16[3,256,384]{2,1,0:T(8,128)(2,1)}, bf16[3,1024,768]{2,1,0:T(8,128)(2,1)}, bf16[3,256,768]{2,1,0:T(8,...) custom-call(bf16[3,256,768]{2,1,0:T(8,128)(2,1)} %refs_0_.1, ...), custom_call_target="tpu_custom_call" | custom-call | flops 6000000000 | bytes 30000000 | tf_op jit(solution)/shard_map/forward_part/pallas_call | solution.py:378
  89.6 3.5 fusion.123
  109.2 56.8 %all-reduce.9.cloned.1.call-done = f32[3,256,768]{2,1,0:T(8,128)} async-done(((f32[3,256,768]{2,1,0:T(8,128)}), f32[3,256,768]{2,1,0:T(8,128)}) %all-reduce.9.cloned.1.call-update) | async-done | bytes 2359312 | tf_op jit(solution)/shard_map/psum | solution.py:485
  172.9 6.6 convert_reduce_fusion
  180.8 3.4 fusion.80
  187.1 4.1 fusion.60
  191.8 4.1 fusion.58
  198.7 54.4 %all-reduce.11.cloned.1.call-done = f32[3,256,768]{2,1,0:T(8,128)} async-done(((f32[3,256,768]{2,1,0:T(8,128)}), f32[3,256,768]{2,1,0:T(8,128)}) %all-reduce.11.cloned.1.call-update) | async-done | bytes 2359312 | tf_op jit(solution)/shard_map/psum | solution.py:502
  262.6 3.5 fusion.117
  266.2 3.8 fusion.46
  279.4 42.4 %while.14 = (s32[]{:T(128)}, f32[3,256,6,64]{1,3,2,0:T(8,128)}, f32[3,768,6,64]{1,3,2,0:T(8,128)}, f32[3,768,6,64]{1,3,2,0:T(8,128)}, bf16[3,768,6,64]{1,3,2,0:T...) while((s32[]{:T(128)}, f32[3,256,6,64]{1,3,2,0:T(8,128)}, ...), condition=%wide.region_12.13_spmd, body=%wide.region_10.12_spmd.sunk | while | flops 773061120 | bytes 44682364 | solution.py:511
  321.8 6.5 pad_maximum_fusion
  328.3 8.1 %copy.113 = f32[3,768,768]{2,1,0:T(8,128)} copy(f32[3,768,768]{1,2,0:T(8,128)} %pad_maximum_fusion) | data formatting | bytes 14155776 | tf_op jit(solution)/shard_map/concatenate | solution.py:528
  336.4 5.4 broadcast_in_dim.121
  342.5 3.3 constant_dynamic-update-slice_fusion
  346.7 3.9 copy.119
  350.6 8.3 %fusion.94 = bf16[3,256,768]{2,1,0:T(8,128)(2,1)} fusion(bf16[768,1536]{1,0:T(8,128)(2,1)} %get-tuple-element.83, f32[3,256,1536]{2,1,0:T(8,128)} %copy-done.62, f32[1536]{0:T(1024)S(1)} %copy-done.56), kind=kOutput, calls=%fused_computation.133 | convolution fusion | flops 1824325632 | bytes 8263680 | tf_op jit(solution)/shard_map/sbf,fd->sbd/dot_general | solution.py:491
  362.3 4.4 fusion.165
  366.7 57.8 %reduce-scatter.6.cloned.1.call-done = f32[3,256,768]{2,1,0:T(8,128)} async-done(((f32[3,1024,768]{2,1,0:T(8,128)}), f32[3,256,768]{2,1,0:T(8,128)}) %reduce-scatter.6.cloned.1.call-update) | async-done | bytes 2359312 | tf_op jit(solution)/shard_map/reduce_scatter | solution.py:530
  424.6 14.2 %scatter_fusion = f32[768,768]{1,0:T(8,128)} fusion(f32[768,768]{1,0:T(8,128)} %bitcast.267, s32[1536]{0:T(1024)S(1)} %reshape.331, f32[1536,768]{1,0:T(8,128)} %bitcast.269), kind=kCustom, calls=%fused_computation | custom fusion | flops 1179648 | bytes 14161920
  451.4 6.0 bitcast_convert_fusion.1
  458.6 6.2 bitcast_convert_fusion
  466.1 4.4 bitcast_convert_fusion.2
  470.8 4.7 fusion.54
  476.1 4.8 fusion.56
  482.4 33.6 %all-reduce.17.cloned.1.call-done = (bf16[3,256,768]{2,1,0:T(8,128)(2,1)}, bf16[3,256,768]{2,1,0:T(8,128)(2,1)}) async-done(((bf16[3,256,768]{2,1,0:T(8,128)(2,1)}, bf16[3,256,768]{2,1,0:T(8,128)(2,1)}), (bf16[3,256,768]{2,1,0:T(8,128)(2,1)}, bf16[3,256,768]{2,1,0:T(8,128)(2,1)})) %all-reduce.17.cloned.1.call-update) | async-done | bytes 2359312 | tf_op jit(solution)/shard_map/psum | solution.py:492
  521.2 19.7 %reduce-scatter.10.cloned.1.call-done = bf16[384,192]{0,1:T(8,128)(2,1)} async-done(((bf16[384,768]{0,1:T(8,128)(2,1)}), bf16[384,192]{0,1:T(8,128)(2,1)}) %reduce-scatter.10.cloned.1.call-update) | async-done | bytes 147472 | tf_op jit(solution)/shard_map/reduce_scatter | solution.py:541
  540.9 48.9 %reduce-scatter.12.cloned.1.call-done = bf16[192,1536]{1,0:T(8,128)(2,1)} async-done(((bf16[768,1536]{1,0:T(8,128)(2,1)}), bf16[192,1536]{1,0:T(8,128)(2,1)}) %reduce-scatter.12.cloned.1.call-update) | async-done | bytes 589840 | tf_op jit(solution)/shard_map/reduce_scatter | solution.py:541
  589.7 50.0 %reduce-scatter.14.cloned.1.call-done = bf16[1536,192]{0,1:T(8,128)(2,1)} async-done(((bf16[1536,768]{0,1:T(8,128)(2,1)}), bf16[1536,192]{0,1:T(8,128)(2,1)}) %reduce-scatter.14.cloned.1.call-update) | async-done | bytes 589840 | tf_op jit(solution)/shard_map/reduce_scatter | solution.py:541
  639.7 40.4 %reduce-scatter.8.cloned.1.call-done = bf16[192,3,384]{2,0,1:T(8,128)(2,1)} async-done(((bf16[768,3,384]{2,0,1:T(8,128)(2,1)}), bf16[192,3,384]{2,0,1:T(8,128)(2,1)}) %reduce-scatter.8.cloned.1.call-update) | async-done | bytes 442384 | tf_op jit(solution)/shard_map/reduce_scatter | solution.py:541
  680.8 4.4 convert_reduce_fusion.4
  685.2 61.4 %all-reduce = (f32[768]{0:T(1024)}, f32[768]{0:T(1024)}, f32[3,384]{1,0:T(4,128)}, f32[6,256]{1,0:T(8,128)}, f32[6,256]{1,0:T(8,128)}, /*index=5*/f32[768]{0:T(1...) all-reduce(f32[768]{0:T(1024)} %get-tuple-element.138, ...), channel_id=1, replica_groups=mesh['dp'=4,'ctx'=4,'tp'=2] {'dp','ctx'}, use_global_device_ids=true, to_apply=%region_25.26 | all-reduce | flops 10368 | bytes 82944 | tf_op jit(solution)/shard_map/psum | solution.py:537
  (253 shorter events, 136.4 us)
Async XLA Ops:
  7.2 158.9 %all-reduce.9.cloned.1.call-start = ((), (), s32[]{:S(2)}) async-start(), calls=%async_computation.5 | async-start | bytes 4718592 | tf_op jit(solution)/shard_map/psum | solution.py:485
  93.1 160.0 %all-reduce.11.cloned.1.call-start = ((), (), s32[]{:S(2)}) async-start(), calls=%async_computation.6 | async-start | bytes 4718592 | tf_op jit(solution)/shard_map/psum | solution.py:502
  104.5 61.5 %copy-start.3 = (bf16[3,256,768]{2,1,0:T(8,128)(2,1)S(1)}, bf16[3,256,768]{2,1,0:T(8,128)(2,1)}, u32[]{:S(2)}) copy-start(bf16[3,256,768]{2,1,0:T(8,128)(2,1)} %refs_0_.1) | copy-start | bytes 3538948
  104.5 61.5 %copy-start.50 = (f32[768]{0:T(1024)S(1)}, f32[768]{0:T(1024)}, u32[]{:S(2)}) copy-start(f32[768]{0:T(1024)} %param.31) | copy-start | bytes 9220
  172.8 6.6 copy-start.62
  184.3 178.0 %all-reduce.13.cloned.1.call-start = ((), (), s32[]{:S(2)}) async-start(), calls=%async_computation.8 | async-start | bytes 2359296 | tf_op jit(solution)/shard_map/psum | solution.py:519
  187.1 4.8 copy-start
  187.1 4.8 copy-start.45
  191.2 4.7 copy-start.23
  195.9 57.1 %copy-start.41 = (f32[768]{0:T(1024)S(1)}, f32[768]{0:T(1024)}, u32[]{:S(2)}) copy-start(f32[768]{0:T(1024)} %param.32) | copy-start | bytes 9220
  279.4 145.2 %reduce-scatter.6.cloned.1.call-start = ((), (), s32[]{:S(2)}) async-start(), calls=%async_computation.7 | async-start | bytes 11796480 | tf_op jit(solution)/shard_map/reduce_scatter | solution.py:530
  336.4 6.1 copy-start.1
  345.8 4.7 copy-start.56
  345.9 170.2 %all-reduce.17.cloned.1.call-start = ((), (), s32[]{:S(2)}) async-start(), calls=%async_computation.14 | async-start | bytes 4718592 | tf_op jit(solution)/shard_map/psum | solution.py:492
  350.6 8.3 %copy-start.15 = (bf16[3,256,384]{1,2,0:T(8,128)(2,1)S(1)}, bf16[3,256,384]{1,2,0:T(8,128)(2,1)}, u32[]{:S(2)}) copy-start(bf16[3,256,384]{1,2,0:T(8,128)(2,1)} %copy.111) | copy-start | bytes 1769476
  350.6 8.3 %copy-start.30 = (f32[6,3,256]{2,0,1:T(8,128)S(1)}, f32[6,3,256]{2,0,1:T(8,128)}, u32[]{:S(2)}) copy-start(f32[6,3,256]{2,0,1:T(8,128)} %copy-done.29) | copy-start | bytes 55300
  350.6 8.3 %copy-start.33 = (f32[6,3,256]{2,0,1:T(8,128)S(1)}, f32[6,3,256]{2,0,1:T(8,128)}, u32[]{:S(2)}) copy-start(f32[6,3,256]{2,0,1:T(8,128)} %copy-done.32) | copy-start | bytes 55300
  350.6 8.3 %copy-start.49 = (f32[6,256]{1,0:T(8,128)S(1)}, f32[6,256]{1,0:T(8,128)}, u32[]{:S(2)}) copy-start(f32[6,256]{1,0:T(8,128)} %refs_11_.1) | copy-start | bytes 18436
  350.6 8.3 %copy-start.54 = (f32[3,256,6,64]{1,3,2,0:T(8,128)S(1)}, f32[3,256,6,64]{1,3,2,0:T(8,128)}, u32[]{:S(2)}) copy-start(f32[3,256,6,64]{1,3,2,0:T(8,128)} %get-tuple-element.87) | copy-start | bytes 3538948
  447.1 4.3 copy-start.59
  447.1 93.8 %reduce-scatter.10.cloned.1.call-start = ((), (), s32[]{:S(2)}) async-start(), calls=%async_computation.10 | async-start | bytes 737280 | tf_op jit(solution)/shard_map/reduce_scatter | solution.py:541
  451.1 138.7 %reduce-scatter.12.cloned.1.call-start = ((), (), s32[]{:S(2)}) async-start(), calls=%async_computation.11 | async-start | bytes 2949120 | tf_op jit(solution)/shard_map/reduce_scatter | solution.py:541
  457.4 182.3 %reduce-scatter.14.cloned.1.call-start = ((), (), s32[]{:S(2)}) async-start(), calls=%async_computation.12 | async-start | bytes 2949120 | tf_op jit(solution)/shard_map/reduce_scatter | solution.py:541
  464.8 215.2 %reduce-scatter.8.cloned.1.call-start = ((), (), s32[]{:S(2)}) async-start(), calls=%async_computation.9 | async-start | bytes 2211840 | tf_op jit(solution)/shard_map/reduce_scatter | solution.py:541
  466.1 4.7 copy-start.43
  470.5 278.7 %all-reduce.15.cloned.1.call-start = ((), (), s32[]{:S(2)}) async-start(), calls=%async_computation.13 | async-start | bytes 3538944 | tf_op jit(solution)/shard_map/psum | solution.py:542
  470.8 5.3 copy-start.31
  476.1 5.5 copy-start.13
  476.1 5.5 copy-start.17
  476.1 40.0 %copy-start.4 = (bf16[3,256,768]{2,1,0:T(8,128)(2,1)S(1)}, bf16[3,256,768]{2,1,0:T(8,128)(2,1)}, u32[]{:S(2)}) copy-start(bf16[3,256,768]{2,1,0:T(8,128)(2,1)} %refs_0_.1) | copy-start | bytes 3538948
  476.1 40.0 %copy-start.34 = (f32[768]{0:T(1024)S(1)}, f32[768]{0:T(1024)}, u32[]{:S(2)}) copy-start(f32[768]{0:T(1024)} %param.24) | copy-start | bytes 9220
  749.1 5.9 copy-start.21
  (44 other events, 99.9 us)
Sparse Core Ops, SparseCore 0:
  93.2 72.7 all-reduce.8
  184.4 68.6 all-reduce.10
  279.5 37.2 all-reduce.12
  346.0 78.5 reduce-scatter.5
  447.2 68.7 all-reduce.16
  518.9 21.9 reduce-scatter.9
  543.3 46.4 reduce-scatter.11
  592.1 47.5 reduce-scatter.13
  642.1 37.8 reduce-scatter.7
  682.5 46.5 all-reduce.14
